TPU v7x, 32 devices: a whole 2x2x4 slice. The times are simulated.
32 devices in a mesh: day: 2 (over x), sta: 16 (over z, y, core).
Axes of the slice: x: 2, y: 2, z: 4, core: 2. Of those that a mesh axis runs over, the one named last changes fastest.
Arguments:
- spectra: bfloat16 [256, 4, 2, 8192], P(('day', 'sta')), parts along dimension 0, may hold values from -6 to 6
- window_mask: int32 [256, 4], P(('day', 'sta')), parts along dimension 0, may hold values from 0 to 1, as said below
- pair_slots: int32 [32, 2], P('sta'), may hold values from -1 to 15, as said below
Outputs:
- stacks: bfloat16 [64, 8, 8, 1024], P(('day', 'sta')), parts along dimension 0
There are 2 independent parts, one for each index of `day`. A program takes and returns all parts, laid end to end along the dimension named above; an argument that names none is the same for every part. Nothing has to cross between parts.
Inputs may be any that keep to these rules, and one draw needn't show every extreme that they name: `pair_slots`: row o * 2 + c is slot c of owner block o: either (-1, -1), an empty slot, or two blocks a <= b, each within 2 blocks of o. An owner's live slots come before its empty ones; some owner fills all 2 slots and some owner has none. `window_mask`: in every draw some stations have no valid window at all.
All inputs are finite; a program needn't handle non-finite values.
Results may differ from a plain program's by a relative error of at most 0.0047.
Values may be sent and summed in bfloat16 or wider, within the bound.
A program may use at most 128 MiB of HBM per device.

v0:
```python
import functools
import math

import jax
import jax.numpy as jnp
import numpy as np
from jax import lax
from jax.experimental import pallas as pl
from jax.experimental.pallas import tpu as pltpu
from jax.sharding import PartitionSpec as P

LAGS = 1024
REACH = 2
GROUP = 4
CHUNKS = 4
LANES = 128
FINE = 32
MESH = pl.DeviceIdType.MESH


def phase_tables(steps, frequency_values, lag_count):
    lag = np.arange(lag_count, dtype=np.int64) - lag_count // 2
    phase = np.mod(np.asarray(steps, np.int64)[:, None] * lag[None, :], 2 * frequency_values)
    angle = phase.astype(np.float64) * (math.pi / frequency_values)
    return np.stack([np.cos(angle), np.sin(angle)]).astype(np.float32)


def kernel(
    dims,
    spec_ref,
    mask_ref,
    pair_ref,
    rank_table,
    coarse_table,
    fine_table,
    out_ref,
    held,
    meta,
    slot_smem,
    wide,
    cross,
    table,
    total,
    from_core,
    to_row,
    from_row,
    local_sem,
    group_send,
    group_recv,
    line_send,
    line_recv,
    meta_send,
    meta_recv,
    meta_line_send,
    meta_line_recv,
    sum_send,
    sum_recv,
):
    stations, windows, slots, freqs, lags, groups = dims
    rows = stations * windows * 2
    per_station = windows * 2
    pairs = stations * stations
    held_blocks = GROUP + 2 * REACH
    share = freqs // GROUP
    chunk = share // CHUNKS
    tiles = chunk // LANES

    me = lax.axis_index("sta")
    group = me // GROUP
    rank = me % GROUP
    core = rank % 2
    side = rank // 2
    first = group * GROUP
    has_before = group > 0
    has_behind = group < groups - 1
    before = me - GROUP
    behind = me + GROUP

    barrier = pltpu.get_barrier_semaphore()
    for step in range(1, GROUP):
        pl.semaphore_signal(
            barrier, inc=1, device_id={"sta": first + (rank + step) % GROUP}, device_id_type=MESH
        )

    @pl.when(has_before)
    def _():
        pl.semaphore_signal(barrier, inc=1, device_id={"sta": before}, device_id_type=MESH)

    @pl.when(has_behind)
    def _():
        pl.semaphore_signal(barrier, inc=1, device_id={"sta": behind}, device_id_type=MESH)

    own = REACH + rank
    lane = lax.broadcasted_iota(jnp.int32, (8, LANES), 1)
    slot_row = jnp.zeros((8, LANES), jnp.int32)
    for slot in range(slots):
        for end in range(2):
            slot_row = jnp.where(lane == slot * 2 + end, pair_ref[slot, end], slot_row)
    meta[own, pl.ds(stations, 8), :] = slot_row
    meta[own, pl.ds(0, stations), :] = jnp.zeros((stations, LANES), jnp.int32)
    meta[own, pl.ds(0, stations), pl.ds(0, windows)] = mask_ref[...]

    neighbours = (GROUP - 1) + has_before.astype(jnp.int32) + has_behind.astype(jnp.int32)
    pl.semaphore_wait(barrier, neighbours)

    def group_meta(step):
        return pltpu.make_async_remote_copy(
            src_ref=meta.at[own],
            dst_ref=meta.at[own],
            send_sem=meta_send.at[step - 1],
            recv_sem=meta_recv.at[step - 1],
            device_id={"sta": first + (rank + step) % GROUP},
            device_id_type=MESH,
        )

    def group_copy(index, step):
        peer = (rank + step) % GROUP
        start = pl.multiple_of(peer * share + index * chunk, LANES)
        return pltpu.make_async_remote_copy(
            src_ref=spec_ref.at[:, pl.ds(start, chunk)],
            dst_ref=held.at[index, own],
            send_sem=group_send.at[index, step - 1],
            recv_sem=group_recv.at[index, step - 1],
            device_id={"sta": first + peer},
            device_id_type=MESH,
        )

    def own_copy(index):
        start = pl.multiple_of(rank * share + index * chunk, LANES)
        return pltpu.make_async_copy(
            spec_ref.at[:, pl.ds(start, chunk)], held.at[index, own], local_sem.at[index]
        )

    def line_copy(index, down):
        source, target, peer = (GROUP, 0, behind) if down else (REACH, GROUP + REACH, before)
        return pltpu.make_async_remote_copy(
            src_ref=held.at[index, pl.ds(source, REACH)],
            dst_ref=held.at[index, pl.ds(target, REACH)],
            send_sem=line_send.at[index, int(down)],
            recv_sem=line_recv.at[index, int(down)],
            device_id={"sta": peer},
            device_id_type=MESH,
        )

    def meta_line(down):
        source, target, peer = (GROUP, 0, behind) if down else (REACH, GROUP + REACH, before)
        return pltpu.make_async_remote_copy(
            src_ref=meta.at[pl.ds(source, REACH)],
            dst_ref=meta.at[pl.ds(target, REACH)],
            send_sem=meta_line_send.at[int(down)],
            recv_sem=meta_line_recv.at[int(down)],
            device_id={"sta": peer},
            device_id_type=MESH,
        )

    steps = (2, 1, 3)
    for step in steps:
        group_meta(step).start()
    for index in range(CHUNKS):
        own_copy(index).start()
        for step in steps:
            group_copy(index, step).start()

    rank_cos = rank_table[0, pl.ds(rank, 1), :]
    rank_sin = rank_table[1, pl.ds(rank, 1), :]

    def fill(coarse, carry):
        step_cos = coarse_table[0, pl.ds(coarse, 1), :]
        step_sin = coarse_table[1, pl.ds(coarse, 1), :]
        base_cos = step_cos * rank_cos - step_sin * rank_sin
        base_sin = step_sin * rank_cos + step_cos * rank_sin
        index = (coarse * FINE) // chunk
        row = pl.multiple_of((coarse * FINE) % chunk, FINE)
        fine_cos = fine_table[0]
        fine_sin = fine_table[1]
        table[index, pl.ds(row, FINE), :] = (base_cos * fine_cos - base_sin * fine_sin).astype(
            jnp.bfloat16
        )
        table[index, pl.ds(chunk + row, FINE), :] = (
            -(base_sin * fine_cos + base_cos * fine_sin)
        ).astype(jnp.bfloat16)
        return carry

    lax.fori_loop(0, share // FINE, fill, 0)

    for step in steps:
        group_meta(step).wait_recv()
    slots_copy = pltpu.make_async_copy(
        meta.at[pl.ds(REACH, GROUP), pl.ds(stations, 8)], slot_smem, local_sem.at[CHUNKS]
    )
    slots_copy.start()

    @pl.when(has_behind)
    def _():
        meta_line(True).start()

    @pl.when(has_before)
    def _():
        meta_line(False).start()

    slots_copy.wait()

    def forward(index):
        own_copy(index).wait()
        for step in steps:
            group_copy(index, step).wait_recv()

        @pl.when(has_behind)
        def _():
            line_copy(index, True).start()

        @pl.when(has_before)
        def _():
            line_copy(index, False).start()

    def place(value):
        local = jnp.where(value < 0, REACH, value - (first - REACH))
        return jnp.clip(local, 0, held_blocks - 1)

    def work(index):
        @pl.when(has_before)
        def _():
            line_copy(index, True).wait_recv()

        @pl.when(has_behind)
        def _():
            line_copy(index, False).wait_recv()

        def widen(block, carry):
            start = pl.multiple_of(block * rows, rows)
            for tile in range(tiles):
                wide[tile, pl.ds(start, rows), :] = held[
                    index, block, :, pl.ds(tile * LANES, LANES)
                ].astype(jnp.float32)
            return carry

        lax.fori_loop(0, held_blocks, widen, 0)

        def slot_cross(place_at, carry):
            slot = place_at % slots
            owner = ((place_at // slots) % 2) * 2 + place_at // (2 * slots)
            left = place(slot_smem[owner, 0, slot * 2]) * rows
            right = place(slot_smem[owner, 0, slot * 2 + 1]) * rows
            out_row = pl.multiple_of(place_at * pairs, pairs)

            def tile_cross(tile, inner):
                column = pl.multiple_of(tile * LANES, LANES)
                right_real = [
                    wide[tile, pl.ds(right + 2 * w, stations, stride=per_station), :]
                    for w in range(windows)
                ]
                right_imag = [
                    wide[tile, pl.ds(right + 2 * w + 1, stations, stride=per_station), :]
                    for w in range(windows)
                ]
                for couple in range(0, stations, 2):
                    reals, imags = [], []
                    for station in (couple, couple + 1):
                        real = imag = None
                        for w in range(windows):
                            at = left + station * per_station + 2 * w
                            left_real = wide[tile, pl.ds(at, 1), :]
                            left_imag = wide[tile, pl.ds(at + 1, 1), :]
                            real_term = left_real * right_real[w] + left_imag * right_imag[w]
                            imag_term = left_imag * right_real[w] - left_real * right_imag[w]
                            real = real_term if real is None else real + real_term
                            imag = imag_term if imag is None else imag + imag_term
                        reals.append(real)
                        imags.append(imag)
                    at_row = out_row + couple * stations
                    cross[pl.ds(pl.multiple_of(at_row, 16), 16), pl.ds(column, LANES)] = (
                        jnp.concatenate(reals, axis=0).astype(jnp.bfloat16)
                    )
                    cross[
                        pl.ds(pl.multiple_of(at_row, 16), 16), pl.ds(chunk + column, LANES)
                    ] = jnp.concatenate(imags, axis=0).astype(jnp.bfloat16)
                return inner

            return lax.fori_loop(0, tiles, tile_cross, carry)

        lax.fori_loop(0, GROUP * slots, slot_cross, 0)

        half = 2 * slots * pairs
        width = 256

        def multiply(at, carry):
            column = pl.multiple_of(at * width, width)
            for k in range(2):
                product = jnp.dot(
                    cross[pl.ds(k * half, half), :],
                    table[index, :, pl.ds(column, width)],
                    preferred_element_type=jnp.float32,
                )
                if index > 0:
                    product = product + total[k, :, pl.ds(column, width)]
                total[k, :, pl.ds(column, width)] = product
            return carry

        lax.fori_loop(0, lags // width, multiply, 0)

    forward(0)
    for index in range(CHUNKS):
        if index + 1 < CHUNKS:
            forward(index + 1)
        work(index)

    mine = slots * pairs
    core_copy = pltpu.make_async_remote_copy(
        src_ref=total.at[1 - core],
        dst_ref=from_core,
        send_sem=sum_send.at[0],
        recv_sem=sum_recv.at[0],
        device_id={"sta": first + side * 2 + 1 - core},
        device_id_type=MESH,
    )
    core_copy.start()
    core_copy.wait_recv()
    other = pl.multiple_of((1 - side) * mine, mine)
    to_row[...] = (total[core, pl.ds(other, mine), :] + from_core[pl.ds(other, mine), :]).astype(
        jnp.bfloat16
    )
    row_copy = pltpu.make_async_remote_copy(
        src_ref=to_row,
        dst_ref=from_row,
        send_sem=sum_send.at[1],
        recv_sem=sum_recv.at[1],
        device_id={"sta": first + (rank + 2) % GROUP},
        device_id_type=MESH,
    )
    row_copy.start()

    @pl.when(has_before)
    def _():
        meta_line(True).wait_recv()

    @pl.when(has_behind)
    def _():
        meta_line(False).wait_recv()

    scales = []
    for slot in range(slots):
        left_mask = meta[place(pair_ref[slot, 0]), pl.ds(0, stations), :].astype(jnp.float32)
        right_mask = meta[place(pair_ref[slot, 1]), pl.ds(0, stations), :].astype(jnp.float32)
        counts = jnp.concatenate(
            [
                jnp.sum(left_mask[p : p + 1] * right_mask, axis=1, keepdims=True)
                for p in range(stations)
            ],
            axis=0,
        )
        live = jnp.where(pair_ref[slot, 0] >= 0, 1.0, 0.0)
        scales.append(live / (math.sqrt(freqs) * jnp.maximum(counts, 1.0)))

    row_copy.wait_recv()
    for slot in range(slots):
        start = pl.multiple_of(side * mine + slot * pairs, pairs)
        running = (
            total[core, pl.ds(start, pairs), :]
            + from_core[pl.ds(start, pairs), :]
            + from_row[pl.ds(slot * pairs, pairs), :].astype(jnp.float32)
        )
        out_ref[pl.ds(slot * pairs, pairs), :] = (running * scales[slot]).astype(jnp.bfloat16)

    core_copy.wait_send()
    row_copy.wait_send()
    for step in steps:
        group_meta(step).wait_send()
        for index in range(CHUNKS):
            group_copy(index, step).wait_send()

    @pl.when(has_behind)
    def _():
        meta_line(True).wait_send()
        for index in range(CHUNKS):
            line_copy(index, True).wait_send()

    @pl.when(has_before)
    def _():
        meta_line(False).wait_send()
        for index in range(CHUNKS):
            line_copy(index, False).wait_send()


def shards(groups, spectra, window_mask, pair_slots):
    stations, windows, _, freqs = spectra.shape
    slots = pair_slots.shape[0]
    rows = stations * windows * 2
    pairs = stations * stations
    held_blocks = GROUP + 2 * REACH
    share = freqs // GROUP
    chunk = share // CHUNKS
    masked = spectra * window_mask[:, :, None, None].astype(spectra.dtype)
    rank_table = phase_tables(np.arange(GROUP) * share, freqs, LAGS)
    coarse_table = phase_tables(np.arange(share // FINE) * FINE, freqs, LAGS)
    fine_table = phase_tables(np.arange(FINE), freqs, LAGS)
    vmem = pl.BlockSpec(memory_space=pltpu.VMEM)
    dma = pltpu.SemaphoreType.DMA
    dims = (stations, windows, slots, freqs, LAGS, groups)
    flops = 2 * GROUP * slots * pairs * 2 * share * LAGS
    out = pl.pallas_call(
        functools.partial(kernel, dims),
        out_shape=jax.ShapeDtypeStruct((slots * pairs, LAGS), jnp.bfloat16),
        in_specs=[vmem, vmem, pl.BlockSpec(memory_space=pltpu.SMEM), vmem, vmem, vmem],
        out_specs=vmem,
        scratch_shapes=[
            pltpu.VMEM((CHUNKS, held_blocks, rows, chunk), jnp.bfloat16),
            pltpu.VMEM((held_blocks, stations + 8, LANES), jnp.int32),
            pltpu.SMEM((GROUP, 8, LANES), jnp.int32),
            pltpu.VMEM((chunk // LANES, held_blocks * rows, LANES), jnp.float32),
            pltpu.VMEM((GROUP * slots * pairs, 2 * chunk), jnp.bfloat16),
            pltpu.VMEM((CHUNKS, 2 * chunk, LAGS), jnp.bfloat16),
            pltpu.VMEM((2, 2 * slots * pairs, LAGS), jnp.float32),
            pltpu.VMEM((2 * slots * pairs, LAGS), jnp.float32),
            pltpu.VMEM((slots * pairs, LAGS), jnp.bfloat16),
            pltpu.VMEM((slots * pairs, LAGS), jnp.bfloat16),
            dma((CHUNKS + 1,)),
            dma((CHUNKS, GROUP - 1)),
            dma((CHUNKS, GROUP - 1)),
            dma((CHUNKS, 2)),
            dma((CHUNKS, 2)),
            dma((GROUP - 1,)),
            dma((GROUP - 1,)),
            dma((2,)),
            dma((2,)),
            dma((2,)),
            dma((2,)),
        ],
        compiler_params=pltpu.CompilerParams(
            collective_id=0, has_side_effects=True, vmem_limit_bytes=48 * 1024 * 1024
        ),
        cost_estimate=pl.CostEstimate(flops=flops, bytes_accessed=4 * 2**20, transcendentals=0),
    )(
        masked.reshape(rows, freqs),
        window_mask,
        pair_slots,
        jnp.asarray(rank_table),
        jnp.asarray(coarse_table),
        jnp.asarray(fine_table),
    )
    return out.reshape(slots, stations, stations, LAGS)


def solution(mesh):
    placed = (P(("day", "sta"), None, None, None), P(("day", "sta"), None), P("sta", None))
    groups = mesh.shape["sta"] // GROUP
    return jax.shard_map(
        functools.partial(shards, groups),
        mesh=mesh,
        in_specs=placed,
        out_specs=P(("day", "sta"), None, None, None),
        check_vma=False,
    )
```

profile of v0, /device:TPU:0, one launch (start us, length us, event | category | flops | bytes accessed | tf_op | source)
XLA Modules:
  0.0 45.7 jit_solution(15676601819281741975)
XLA Ops:
  0.0 0.7 %convert_element_type.4 = bf16[8,4]{0,1:T(4,128)(2,1)S(1)} convert(s32[8,4]{0,1:T(4,128)} %param.7) | non-fusion elementwise | flops 32 | bytes 192 | tf_op jit(solution)/shard_map/convert_element_type | solution.py:392
  0.7 0.1 copy.7
  0.8 2.2 %broadcast_multiply_fusion = bf16[8,4,2,8192]{3,2,1,0:T(2,128)(2,1)S(1)} fusion(bf16[8,4,2,8192]{3,2,1,0:T(2,128)(2,1)} %param.6, bf16[8,4]{1,0:T(8,128)(2,1)S(1)} %copy.7), kind=kLoop, calls=%fused_computation | loop fusion | flops 524288 | bytes 2097216 | tf_op jit(solution)/shard_map/mul | solution.py:392
  3.0 0.0 copy-start.4
  3.0 0.0 copy-start.1
  3.0 0.0 copy-start.2
  3.0 0.0 copy-start.3
  3.0 0.4 reshape.8.spec_ref
  3.5 0.2 copy-done.4
  3.7 0.0 copy-start
  3.7 0.1 copy.8.mask_ref
  3.8 0.3 copy-done.1
  4.0 0.1 copy-done.2
  4.1 0.0 copy-done.3
  4.1 0.3 copy-done
  4.4 40.6 %shard_map.64 = bf16[128,1024]{1,0:T(8,128)(2,1)S(1)} custom-call(bf16[64,8192]{1,0:T(8,128)(2,1)S(1)} %reshape.8.spec_ref, s32[8,4]{1,0:T(8,128)S(1)} %copy.8.mask_ref, s32[2,2]{1,0:T(2,128)S(1)} %copy-done, f32[2,4,1024]{2,1,0:T(4,128)S(1)} %copy-done.3, f32[2,64,1024]{2,1,0:T(8,128)S(1)} %copy-done.1, f32[2,32,1024]{2,1,0:T(8,128)S(1)} %copy-done.2), custom_call_target="tpu_custom_call" | custom-call | flops 4294967296 | bytes 4194304 | tf_op jit(solution)/shard_map/pallas_call | solution.py:400
  45.0 0.7 %copy.10 = bf16[2,8,8,1024]{3,2,1,0:T(8,128)(2,1)} copy(bf16[2,8,8,1024]{3,2,1,0:T(8,128)(2,1)S(1)} %bitcast.1) | data formatting | bytes 524288
Async XLA Ops:
  3.0 0.7 %copy-start.4 = (s32[8,4]{0,1:T(4,128)S(1)}, s32[8,4]{0,1:T(4,128)}, u32[]{:S(2)}) copy-start(s32[8,4]{0,1:T(4,128)} %param.7) | copy-start | bytes 388
  3.0 1.0 %copy-start.1 = (f32[2,64,1024]{2,1,0:T(8,128)S(1)}, f32[2,64,1024]{2,1,0:T(8,128)}, u32[]{:S(2)}) copy-start(f32[2,64,1024]{2,1,0:T(8,128)} %constant.7.clone.coarse_table) | copy-start | bytes 1572868
  3.0 1.1 %copy-start.2 = (f32[2,32,1024]{2,1,0:T(8,128)S(1)}, f32[2,32,1024]{2,1,0:T(8,128)}, u32[]{:S(2)}) copy-start(f32[2,32,1024]{2,1,0:T(8,128)} %constant.8.clone.fine_table) | copy-start | bytes 786436
  3.0 1.1 %copy-start.3 = (f32[2,4,1024]{2,1,0:T(4,128)S(1)}, f32[2,4,1024]{2,1,0:T(4,128)}, u32[]{:S(2)}) copy-start(f32[2,4,1024]{2,1,0:T(4,128)} %constant.6.clone.rank_table) | copy-start | bytes 98308
  3.7 0.7 %copy-start = (s32[2,2]{1,0:T(2,128)S(1)}, s32[2,2]{1,0:T(2,128)}, u32[]{:S(2)}) copy-start(s32[2,2]{1,0:T(2,128)} %pair_ref.1) | copy-start | bytes 52
where the time goes:
time: 45.9 us; the launch traced here: 45.7 us
  Pallas kernels  40.6 us (88%)
  other arithmetic  2.88 us (6%)
  local copies, waits for them, and re-layouts  2.19 us (5%)
    pallas_call x1, Pallas kernels, shards(): pl.pallas_call(functools.partial(kernel, dims), out_shape=jax.ShapeDtypeS...  40.6 us
    mul x1, other arithmetic, shards(): masked = spectra * window_mask[:, :, None, None].astype(spectra.dtype)  2.2 us
    unnamed x12, local copies, waits for them, and re-layouts  1.65 us

commit v1 on v0

--- a/solution.py
+++ b/solution.py
@@ -27,18 +27,21 @@
 
 def kernel(
     dims,
-    spec_ref,
+    raw_ref,
     mask_ref,
     pair_ref,
     rank_table,
     coarse_table,
     fine_table,
     out_ref,
+    spec_ref,
+    mask_rows,
     held,
     meta,
     slot_smem,
     wide,
-    cross,
+    cross_even,
+    cross_odd,
     table,
     total,
     from_core,
@@ -53,8 +56,10 @@
     meta_recv,
     meta_line_send,
     meta_line_recv,
-    sum_send,
-    sum_recv,
+    core_send,
+    core_recv,
+    row_send,
+    row_recv,
 ):
     stations, windows, slots, freqs, lags, groups = dims
     rows = stations * windows * 2
@@ -99,6 +104,20 @@
     meta[own, pl.ds(stations, 8), :] = slot_row
     meta[own, pl.ds(0, stations), :] = jnp.zeros((stations, LANES), jnp.int32)
     meta[own, pl.ds(0, stations), pl.ds(0, windows)] = mask_ref[...]
+
+    for w in range(windows):
+        valid = jnp.broadcast_to(
+            mask_ref[:, pl.ds(w, 1)].astype(jnp.float32), (stations, LANES)
+        )
+        for part in range(2):
+            mask_rows[pl.ds(2 * w + part, stations, stride=per_station), :] = valid
+
+    def mask_tile(tile, carry):
+        column = pl.ds(pl.multiple_of(tile * LANES, LANES), LANES)
+        spec_ref[:, column] = raw_ref[:, column] * mask_rows[...].astype(jnp.bfloat16)
+        return carry
+
+    lax.fori_loop(0, freqs // LANES, mask_tile, 0, unroll=4)
 
     neighbours = (GROUP - 1) + has_before.astype(jnp.int32) + has_behind.astype(jnp.int32)
     pl.semaphore_wait(barrier, neighbours)
@@ -217,6 +236,20 @@
         local = jnp.where(value < 0, REACH, value - (first - REACH))
         return jnp.clip(local, 0, held_blocks - 1)
 
+    half = 2 * slots * pairs
+    width = lags // (2 * slots)
+    cross_of = (cross_even, cross_odd)
+
+    def product(index, k, column):
+        part = jnp.dot(
+            cross_of[index % 2][pl.ds(pl.multiple_of(k * half, half), half), :],
+            table[index, :, pl.ds(column, width)],
+            preferred_element_type=jnp.float32,
+        )
+        if index > 0:
+            part = part + total[k, :, pl.ds(column, width)]
+        total[k, :, pl.ds(column, width)] = part
+
     def work(index):
         @pl.when(has_before)
         def _():
@@ -227,30 +260,33 @@
             line_copy(index, False).wait_recv()
 
         def widen(block, carry):
-            start = pl.multiple_of(block * rows, rows)
             for tile in range(tiles):
-                wide[tile, pl.ds(start, rows), :] = held[
+                wide[tile, block] = held[
                     index, block, :, pl.ds(tile * LANES, LANES)
                 ].astype(jnp.float32)
             return carry
 
         lax.fori_loop(0, held_blocks, widen, 0)
+        cross = cross_of[index % 2]
 
         def slot_cross(place_at, carry):
+            if index > 0:
+                product(
+                    index - 1, place_at % 2, pl.multiple_of((place_at // 2) * width, width)
+                )
             slot = place_at % slots
             owner = ((place_at // slots) % 2) * 2 + place_at // (2 * slots)
-            left = place(slot_smem[owner, 0, slot * 2]) * rows
-            right = place(slot_smem[owner, 0, slot * 2 + 1]) * rows
+            left = place(slot_smem[owner, 0, slot * 2])
+            right = place(slot_smem[owner, 0, slot * 2 + 1])
             out_row = pl.multiple_of(place_at * pairs, pairs)
-
-            def tile_cross(tile, inner):
-                column = pl.multiple_of(tile * LANES, LANES)
+            for tile in range(tiles):
+                column = tile * LANES
                 right_real = [
-                    wide[tile, pl.ds(right + 2 * w, stations, stride=per_station), :]
+                    wide[tile, right, pl.ds(2 * w, stations, stride=per_station), :]
                     for w in range(windows)
                 ]
                 right_imag = [
-                    wide[tile, pl.ds(right + 2 * w + 1, stations, stride=per_station), :]
+                    wide[tile, right, pl.ds(2 * w + 1, stations, stride=per_station), :]
                     for w in range(windows)
                 ]
                 for couple in range(0, stations, 2):
@@ -258,45 +294,25 @@
                     for station in (couple, couple + 1):
                         real = imag = None
                         for w in range(windows):
-                            at = left + station * per_station + 2 * w
-                            left_real = wide[tile, pl.ds(at, 1), :]
-                            left_imag = wide[tile, pl.ds(at + 1, 1), :]
+                            at = station * per_station + 2 * w
+                            left_real = wide[tile, left, pl.ds(at, 1), :]
+                            left_imag = wide[tile, left, pl.ds(at + 1, 1), :]
                             real_term = left_real * right_real[w] + left_imag * right_imag[w]
                             imag_term = left_imag * right_real[w] - left_real * right_imag[w]
                             real = real_term if real is None else real + real_term
                             imag = imag_term if imag is None else imag + imag_term
                         reals.append(real)
                         imags.append(imag)
-                    at_row = out_row + couple * stations
-                    cross[pl.ds(pl.multiple_of(at_row, 16), 16), pl.ds(column, LANES)] = (
-                        jnp.concatenate(reals, axis=0).astype(jnp.bfloat16)
+                    at_row = pl.ds(pl.multiple_of(out_row + couple * stations, 16), 16)
+                    cross[at_row, pl.ds(column, LANES)] = jnp.concatenate(reals, axis=0).astype(
+                        jnp.bfloat16
                     )
-                    cross[
-                        pl.ds(pl.multiple_of(at_row, 16), 16), pl.ds(chunk + column, LANES)
-                    ] = jnp.concatenate(imags, axis=0).astype(jnp.bfloat16)
-                return inner
-
-            return lax.fori_loop(0, tiles, tile_cross, carry)
+                    cross[at_row, pl.ds(chunk + column, LANES)] = jnp.concatenate(
+                        imags, axis=0
+                    ).astype(jnp.bfloat16)
+            return carry
 
         lax.fori_loop(0, GROUP * slots, slot_cross, 0)
-
-        half = 2 * slots * pairs
-        width = 256
-
-        def multiply(at, carry):
-            column = pl.multiple_of(at * width, width)
-            for k in range(2):
-                product = jnp.dot(
-                    cross[pl.ds(k * half, half), :],
-                    table[index, :, pl.ds(column, width)],
-                    preferred_element_type=jnp.float32,
-                )
-                if index > 0:
-                    product = product + total[k, :, pl.ds(column, width)]
-                total[k, :, pl.ds(column, width)] = product
-            return carry
-
-        lax.fori_loop(0, lags // width, multiply, 0)
 
     forward(0)
     for index in range(CHUNKS):
@@ -305,29 +321,49 @@
         work(index)
 
     mine = slots * pairs
-    core_copy = pltpu.make_async_remote_copy(
-        src_ref=total.at[1 - core],
-        dst_ref=from_core,
-        send_sem=sum_send.at[0],
-        recv_sem=sum_recv.at[0],
-        device_id={"sta": first + side * 2 + 1 - core},
-        device_id_type=MESH,
-    )
-    core_copy.start()
-    core_copy.wait_recv()
+    pieces = lags // width
+
+    def core_copy(piece):
+        column = pl.ds(pl.multiple_of(piece * width, width), width)
+        return pltpu.make_async_remote_copy(
+            src_ref=total.at[1 - core, :, column],
+            dst_ref=from_core.at[:, column],
+            send_sem=core_send.at[piece],
+            recv_sem=core_recv.at[piece],
+            device_id={"sta": first + side * 2 + 1 - core},
+            device_id_type=MESH,
+        )
+
+    def row_copy(piece):
+        column = pl.ds(pl.multiple_of(piece * width, width), width)
+        return pltpu.make_async_remote_copy(
+            src_ref=to_row.at[:, column],
+            dst_ref=from_row.at[:, column],
+            send_sem=row_send.at[piece],
+            recv_sem=row_recv.at[piece],
+            device_id={"sta": first + (rank + 2) % GROUP},
+            device_id_type=MESH,
+        )
+
+    def last_of_partner(piece, carry):
+        product(CHUNKS - 1, 1 - core, pl.multiple_of(piece * width, width))
+        core_copy(piece).start()
+        return carry
+
+    lax.fori_loop(0, pieces, last_of_partner, 0)
     other = pl.multiple_of((1 - side) * mine, mine)
-    to_row[...] = (total[core, pl.ds(other, mine), :] + from_core[pl.ds(other, mine), :]).astype(
-        jnp.bfloat16
-    )
-    row_copy = pltpu.make_async_remote_copy(
-        src_ref=to_row,
-        dst_ref=from_row,
-        send_sem=sum_send.at[1],
-        recv_sem=sum_recv.at[1],
-        device_id={"sta": first + (rank + 2) % GROUP},
-        device_id_type=MESH,
-    )
-    row_copy.start()
+
+    def last_of_own(piece, carry):
+        column = pl.ds(pl.multiple_of(piece * width, width), width)
+        product(CHUNKS - 1, core, pl.multiple_of(piece * width, width))
+        core_copy(piece).wait_recv()
+        to_row[:, column] = (
+            total[core, pl.ds(other, mine), column] + from_core[pl.ds(other, mine), column]
+        ).astype(jnp.bfloat16)
+        row_copy(piece).start()
+        return carry
+
+    lax.fori_loop(0, pieces, last_of_own, 0)
 
     @pl.when(has_before)
     def _():
@@ -351,18 +387,26 @@
         live = jnp.where(pair_ref[slot, 0] >= 0, 1.0, 0.0)
         scales.append(live / (math.sqrt(freqs) * jnp.maximum(counts, 1.0)))
 
-    row_copy.wait_recv()
-    for slot in range(slots):
-        start = pl.multiple_of(side * mine + slot * pairs, pairs)
-        running = (
-            total[core, pl.ds(start, pairs), :]
-            + from_core[pl.ds(start, pairs), :]
-            + from_row[pl.ds(slot * pairs, pairs), :].astype(jnp.float32)
-        )
-        out_ref[pl.ds(slot * pairs, pairs), :] = (running * scales[slot]).astype(jnp.bfloat16)
-
-    core_copy.wait_send()
-    row_copy.wait_send()
+    def finish(piece, carry):
+        column = pl.ds(pl.multiple_of(piece * width, width), width)
+        row_copy(piece).wait_recv()
+        for slot in range(slots):
+            start = pl.multiple_of(side * mine + slot * pairs, pairs)
+            running = (
+                total[core, pl.ds(start, pairs), column]
+                + from_core[pl.ds(start, pairs), column]
+                + from_row[pl.ds(slot * pairs, pairs), column].astype(jnp.float32)
+            )
+            out_ref[pl.ds(slot * pairs, pairs), column] = (running * scales[slot]).astype(
+                jnp.bfloat16
+            )
+        return carry
+
+    lax.fori_loop(0, pieces, finish, 0)
+
+    for piece in range(pieces):
+        core_copy(piece).wait_send()
+        row_copy(piece).wait_send()
     for step in steps:
         group_meta(step).wait_send()
         for index in range(CHUNKS):
@@ -389,7 +433,6 @@
     held_blocks = GROUP + 2 * REACH
     share = freqs // GROUP
     chunk = share // CHUNKS
-    masked = spectra * window_mask[:, :, None, None].astype(spectra.dtype)
     rank_table = phase_tables(np.arange(GROUP) * share, freqs, LAGS)
     coarse_table = phase_tables(np.arange(share // FINE) * FINE, freqs, LAGS)
     fine_table = phase_tables(np.arange(FINE), freqs, LAGS)
@@ -403,10 +446,13 @@
         in_specs=[vmem, vmem, pl.BlockSpec(memory_space=pltpu.SMEM), vmem, vmem, vmem],
         out_specs=vmem,
         scratch_shapes=[
+            pltpu.VMEM((rows, freqs), jnp.bfloat16),
+            pltpu.VMEM((rows, LANES), jnp.float32),
             pltpu.VMEM((CHUNKS, held_blocks, rows, chunk), jnp.bfloat16),
             pltpu.VMEM((held_blocks, stations + 8, LANES), jnp.int32),
             pltpu.SMEM((GROUP, 8, LANES), jnp.int32),
-            pltpu.VMEM((chunk // LANES, held_blocks * rows, LANES), jnp.float32),
+            pltpu.VMEM((chunk // LANES, held_blocks, rows, LANES), jnp.float32),
+            pltpu.VMEM((GROUP * slots * pairs, 2 * chunk), jnp.bfloat16),
             pltpu.VMEM((GROUP * slots * pairs, 2 * chunk), jnp.bfloat16),
             pltpu.VMEM((CHUNKS, 2 * chunk, LAGS), jnp.bfloat16),
             pltpu.VMEM((2, 2 * slots * pairs, LAGS), jnp.float32),
@@ -422,15 +468,17 @@
             dma((GROUP - 1,)),
             dma((2,)),
             dma((2,)),
-            dma((2,)),
-            dma((2,)),
+            dma((2 * slots,)),
+            dma((2 * slots,)),
+            dma((2 * slots,)),
+            dma((2 * slots,)),
         ],
         compiler_params=pltpu.CompilerParams(
             collective_id=0, has_side_effects=True, vmem_limit_bytes=48 * 1024 * 1024
         ),
         cost_estimate=pl.CostEstimate(flops=flops, bytes_accessed=4 * 2**20, transcendentals=0),
     )(
-        masked.reshape(rows, freqs),
+        spectra.reshape(rows, freqs),
         window_mask,
         pair_slots,
         jnp.asarray(rank_table),

time: 45.9 us -> 43.2 us (0.941)
  other arithmetic: 2.88 us -> 0 us
  local copies, waits for them, and re-layouts: 2.19 us -> 3.02 us
  Pallas kernels: 40.6 us -> 39.9 us
    mul x1 -> x0, other arithmetic: 2.2 us -> none  [shards(): masked = spectra * window_mask[:, :, None, None].astype(spectra.dtype)]
    reshape x1, local copies, waits for them, and re-layouts: 0.44 us -> 1.54 us  [shards(): spectra.reshape(rows, freqs)]
    convert_element_type x1 -> x0, other arithmetic: 0.68 us -> none  [shards(): masked = spectra * window_mask[:, :, None, None].astype(spectra.dtype)]
    pallas_call x1, Pallas kernels: 40.6 us -> 39.9 us  [shards(): pl.pallas_call(functools.partial(kernel, dims), out_shape=jax.ShapeDtypeS...]
    unnamed x12 -> x10, local copies, waits for them, and re-layouts: 1.65 us -> 1.48 us
where the time goes in v1:
time: 43.2 us; the launch traced here: 43 us
  Pallas kernels  39.9 us (92%)
  local copies, waits for them, and re-layouts  3.02 us (7%)
    pallas_call x1, Pallas kernels, shards(): pl.pallas_call(functools.partial(kernel, dims), out_shape=jax.ShapeDtypeS...  39.9 us
    reshape x1, local copies, waits for them, and re-layouts, shards(): spectra.reshape(rows, freqs)  1.54 us
    unnamed x10, local copies, waits for them, and re-layouts  1.48 us

profile of v1, /device:TPU:0, one launch (start us, length us, event | category | flops | bytes accessed | tf_op | source)
XLA Modules:
  0.0 43.0 jit_solution(9601216570460780282)
XLA Ops:
  0.0 0.8 %copy.7.mask_ref = s32[8,4]{1,0:T(8,128)S(1)} copy(s32[8,4]{0,1:T(4,128)} %param.7) | data formatting | bytes 256 | tf_op args[1]
  0.8 0.0 copy-start
  0.8 0.0 copy-start.1
  0.8 0.0 copy-start.2
  0.8 0.0 copy-start.3
  0.8 1.5 %reshape.6.raw_ref = bf16[64,8192]{1,0:T(8,128)(2,1)S(1)} reshape(bf16[8,4,2,8192]{3,2,1,0:T(2,128)(2,1)} %param.6) | data formatting | bytes 2097152 | tf_op jit(solution)/shard_map/reshape | solution.py:481
  2.3 0.0 copy-done
  2.3 0.0 copy-done.1
  2.3 0.0 copy-done.2
  2.3 0.0 copy-done.3
  2.4 39.9 %shard_map.64 = bf16[128,1024]{1,0:T(8,128)(2,1)S(1)} custom-call(bf16[64,8192]{1,0:T(8,128)(2,1)S(1)} %reshape.6.raw_ref, s32[8,4]{1,0:T(8,128)S(1)} %copy.7.mask_ref, s32[2,2]{1,0:T(2,128)S(1)} %copy-done, f32[2,4,1024]{2,1,0:T(4,128)S(1)} %copy-done.3, f32[2,64,1024]{2,1,0:T(8,128)S(1)} %copy-done.1, f32[2,32,1024]{2,1,0:T(8,128)S(1)} %copy-done.2), custom_call_target="tpu_custom_call" | custom-call | flops 4294967296 | bytes 4194304 | tf_op jit(solution)/shard_map/pallas_call | solution.py:443
  42.3 0.7 %copy.9 = bf16[2,8,8,1024]{3,2,1,0:T(8,128)(2,1)} copy(bf16[2,8,8,1024]{3,2,1,0:T(8,128)(2,1)S(1)} %bitcast.1) | data formatting | bytes 524288
Async XLA Ops:
  0.8 1.6 %copy-start = (s32[2,2]{1,0:T(2,128)S(1)}, s32[2,2]{1,0:T(2,128)}, u32[]{:S(2)}) copy-start(s32[2,2]{1,0:T(2,128)} %pair_ref.1) | copy-start | bytes 52
  0.8 1.6 %copy-start.1 = (f32[2,64,1024]{2,1,0:T(8,128)S(1)}, f32[2,64,1024]{2,1,0:T(8,128)}, u32[]{:S(2)}) copy-start(f32[2,64,1024]{2,1,0:T(8,128)} %constant.7.clone.coarse_table) | copy-start | bytes 1572868
  0.8 1.6 %copy-start.2 = (f32[2,32,1024]{2,1,0:T(8,128)S(1)}, f32[2,32,1024]{2,1,0:T(8,128)}, u32[]{:S(2)}) copy-start(f32[2,32,1024]{2,1,0:T(8,128)} %constant.8.clone.fine_table) | copy-start | bytes 786436
  0.8 1.6 %copy-start.3 = (f32[2,4,1024]{2,1,0:T(4,128)S(1)}, f32[2,4,1024]{2,1,0:T(4,128)}, u32[]{:S(2)}) copy-start(f32[2,4,1024]{2,1,0:T(4,128)} %constant.6.clone.rank_table) | copy-start | bytes 98308

commit v2 on v1

--- a/solution.py
+++ b/solution.py
@@ -12,7 +12,7 @@
 LAGS = 1024
 REACH = 2
 GROUP = 4
-CHUNKS = 4
+CHUNKS = 8
 LANES = 128
 FINE = 32
 MESH = pl.DeviceIdType.MESH
@@ -112,12 +112,14 @@
         for part in range(2):
             mask_rows[pl.ds(2 * w + part, stations, stride=per_station), :] = valid
 
-    def mask_tile(tile, carry):
-        column = pl.ds(pl.multiple_of(tile * LANES, LANES), LANES)
-        spec_ref[:, column] = raw_ref[:, column] * mask_rows[...].astype(jnp.bfloat16)
+    def mask_part(part, carry):
+        valid = mask_rows[...].astype(jnp.bfloat16)
+        for tile in range(tiles):
+            column = pl.multiple_of(part * chunk + tile * LANES, LANES)
+            spec_ref[part, :, pl.ds(tile * LANES, LANES)] = raw_ref[:, pl.ds(column, LANES)] * valid
         return carry
 
-    lax.fori_loop(0, freqs // LANES, mask_tile, 0, unroll=4)
+    lax.fori_loop(0, GROUP * CHUNKS, mask_part, 0, unroll=2)
 
     neighbours = (GROUP - 1) + has_before.astype(jnp.int32) + has_behind.astype(jnp.int32)
     pl.semaphore_wait(barrier, neighbours)
@@ -134,9 +136,8 @@
 
     def group_copy(index, step):
         peer = (rank + step) % GROUP
-        start = pl.multiple_of(peer * share + index * chunk, LANES)
         return pltpu.make_async_remote_copy(
-            src_ref=spec_ref.at[:, pl.ds(start, chunk)],
+            src_ref=spec_ref.at[peer * CHUNKS + index],
             dst_ref=held.at[index, own],
             send_sem=group_send.at[index, step - 1],
             recv_sem=group_recv.at[index, step - 1],
@@ -145,9 +146,8 @@
         )
 
     def own_copy(index):
-        start = pl.multiple_of(rank * share + index * chunk, LANES)
         return pltpu.make_async_copy(
-            spec_ref.at[:, pl.ds(start, chunk)], held.at[index, own], local_sem.at[index]
+            spec_ref.at[rank * CHUNKS + index], held.at[index, own], local_sem.at[index]
         )
 
     def line_copy(index, down):
@@ -183,13 +183,13 @@
     rank_cos = rank_table[0, pl.ds(rank, 1), :]
     rank_sin = rank_table[1, pl.ds(rank, 1), :]
 
-    def fill(coarse, carry):
+    def fill(index, step, carry):
+        coarse = index * (chunk // FINE) + step
         step_cos = coarse_table[0, pl.ds(coarse, 1), :]
         step_sin = coarse_table[1, pl.ds(coarse, 1), :]
         base_cos = step_cos * rank_cos - step_sin * rank_sin
         base_sin = step_sin * rank_cos + step_cos * rank_sin
-        index = (coarse * FINE) // chunk
-        row = pl.multiple_of((coarse * FINE) % chunk, FINE)
+        row = pl.multiple_of(step * FINE, FINE)
         fine_cos = fine_table[0]
         fine_sin = fine_table[1]
         table[index, pl.ds(row, FINE), :] = (base_cos * fine_cos - base_sin * fine_sin).astype(
@@ -199,25 +199,6 @@
             -(base_sin * fine_cos + base_cos * fine_sin)
         ).astype(jnp.bfloat16)
         return carry
-
-    lax.fori_loop(0, share // FINE, fill, 0)
-
-    for step in steps:
-        group_meta(step).wait_recv()
-    slots_copy = pltpu.make_async_copy(
-        meta.at[pl.ds(REACH, GROUP), pl.ds(stations, 8)], slot_smem, local_sem.at[CHUNKS]
-    )
-    slots_copy.start()
-
-    @pl.when(has_behind)
-    def _():
-        meta_line(True).start()
-
-    @pl.when(has_before)
-    def _():
-        meta_line(False).start()
-
-    slots_copy.wait()
 
     def forward(index):
         own_copy(index).wait()
@@ -315,30 +296,48 @@
         lax.fori_loop(0, GROUP * slots, slot_cross, 0)
 
     forward(0)
+    for step in steps:
+        group_meta(step).wait_recv()
+    slots_copy = pltpu.make_async_copy(
+        meta.at[pl.ds(REACH, GROUP), pl.ds(stations, 8)], slot_smem, local_sem.at[CHUNKS]
+    )
+    slots_copy.start()
+
+    @pl.when(has_behind)
+    def _():
+        meta_line(True).start()
+
+    @pl.when(has_before)
+    def _():
+        meta_line(False).start()
+
+    slots_copy.wait()
+
     for index in range(CHUNKS):
         if index + 1 < CHUNKS:
             forward(index + 1)
+        lax.fori_loop(0, chunk // FINE, functools.partial(fill, index), 0)
         work(index)
 
     mine = slots * pairs
     pieces = lags // width
 
-    def core_copy(piece):
+    def core_copy(piece, to_side):
         column = pl.ds(pl.multiple_of(piece * width, width), width)
+        start = pl.multiple_of(to_side * mine, mine)
         return pltpu.make_async_remote_copy(
-            src_ref=total.at[1 - core, :, column],
-            dst_ref=from_core.at[:, column],
-            send_sem=core_send.at[piece],
-            recv_sem=core_recv.at[piece],
+            src_ref=total.at[1 - core, pl.ds(start, mine), column],
+            dst_ref=from_core.at[pl.ds(start, mine), column],
+            send_sem=core_send.at[to_side, piece],
+            recv_sem=core_recv.at[to_side, piece],
             device_id={"sta": first + side * 2 + 1 - core},
             device_id_type=MESH,
         )
 
     def row_copy(piece):
-        column = pl.ds(pl.multiple_of(piece * width, width), width)
         return pltpu.make_async_remote_copy(
-            src_ref=to_row.at[:, column],
-            dst_ref=from_row.at[:, column],
+            src_ref=to_row.at[piece],
+            dst_ref=from_row.at[piece],
             send_sem=row_send.at[piece],
             recv_sem=row_recv.at[piece],
             device_id={"sta": first + (rank + 2) % GROUP},
@@ -347,17 +346,19 @@
 
     def last_of_partner(piece, carry):
         product(CHUNKS - 1, 1 - core, pl.multiple_of(piece * width, width))
-        core_copy(piece).start()
+        core_copy(piece, 1 - side).start()
         return carry
 
     lax.fori_loop(0, pieces, last_of_partner, 0)
+    for piece in range(pieces):
+        core_copy(piece, side).start()
     other = pl.multiple_of((1 - side) * mine, mine)
 
     def last_of_own(piece, carry):
         column = pl.ds(pl.multiple_of(piece * width, width), width)
         product(CHUNKS - 1, core, pl.multiple_of(piece * width, width))
-        core_copy(piece).wait_recv()
-        to_row[:, column] = (
+        core_copy(piece, 1 - side).wait_recv()
+        to_row[piece] = (
             total[core, pl.ds(other, mine), column] + from_core[pl.ds(other, mine), column]
         ).astype(jnp.bfloat16)
         row_copy(piece).start()
@@ -389,13 +390,14 @@
 
     def finish(piece, carry):
         column = pl.ds(pl.multiple_of(piece * width, width), width)
+        core_copy(piece, side).wait_recv()
         row_copy(piece).wait_recv()
         for slot in range(slots):
             start = pl.multiple_of(side * mine + slot * pairs, pairs)
             running = (
                 total[core, pl.ds(start, pairs), column]
                 + from_core[pl.ds(start, pairs), column]
-                + from_row[pl.ds(slot * pairs, pairs), column].astype(jnp.float32)
+                + from_row[piece, pl.ds(slot * pairs, pairs), :].astype(jnp.float32)
             )
             out_ref[pl.ds(slot * pairs, pairs), column] = (running * scales[slot]).astype(
                 jnp.bfloat16
@@ -405,7 +407,8 @@
     lax.fori_loop(0, pieces, finish, 0)
 
     for piece in range(pieces):
-        core_copy(piece).wait_send()
+        core_copy(piece, side).wait_send()
+        core_copy(piece, 1 - side).wait_send()
         row_copy(piece).wait_send()
     for step in steps:
         group_meta(step).wait_send()
@@ -446,7 +449,7 @@
         in_specs=[vmem, vmem, pl.BlockSpec(memory_space=pltpu.SMEM), vmem, vmem, vmem],
         out_specs=vmem,
         scratch_shapes=[
-            pltpu.VMEM((rows, freqs), jnp.bfloat16),
+            pltpu.VMEM((GROUP * CHUNKS, rows, chunk), jnp.bfloat16),
             pltpu.VMEM((rows, LANES), jnp.float32),
             pltpu.VMEM((CHUNKS, held_blocks, rows, chunk), jnp.bfloat16),
             pltpu.VMEM((held_blocks, stations + 8, LANES), jnp.int32),
@@ -457,8 +460,8 @@
             pltpu.VMEM((CHUNKS, 2 * chunk, LAGS), jnp.bfloat16),
             pltpu.VMEM((2, 2 * slots * pairs, LAGS), jnp.float32),
             pltpu.VMEM((2 * slots * pairs, LAGS), jnp.float32),
-            pltpu.VMEM((slots * pairs, LAGS), jnp.bfloat16),
-            pltpu.VMEM((slots * pairs, LAGS), jnp.bfloat16),
+            pltpu.VMEM((2 * slots, slots * pairs, LAGS // (2 * slots)), jnp.bfloat16),
+            pltpu.VMEM((2 * slots, slots * pairs, LAGS // (2 * slots)), jnp.bfloat16),
             dma((CHUNKS + 1,)),
             dma((CHUNKS, GROUP - 1)),
             dma((CHUNKS, GROUP - 1)),
@@ -468,8 +471,8 @@
             dma((GROUP - 1,)),
             dma((2,)),
             dma((2,)),
-            dma((2 * slots,)),
-            dma((2 * slots,)),
+            dma((2, 2 * slots)),
+            dma((2, 2 * slots)),
             dma((2 * slots,)),
             dma((2 * slots,)),
         ],

time: 43.2 us -> 46.3 us (1.072)
  Pallas kernels: 39.9 us -> 43 us
    pallas_call x1, Pallas kernels: 39.9 us -> 43 us  [shards(): pl.pallas_call(functools.partial(kernel, dims), out_shape=jax.ShapeDtypeS...]
where the time goes in v2:
time: 46.3 us; the launch traced here: 46.1 us
  Pallas kernels  43 us (93%)
  local copies, waits for them, and re-layouts  3.02 us (7%)
    pallas_call x1, Pallas kernels, shards(): pl.pallas_call(functools.partial(kernel, dims), out_shape=jax.ShapeDtypeS...  43 us
    reshape x1, local copies, waits for them, and re-layouts, shards(): spectra.reshape(rows, freqs)  1.54 us
    unnamed x10, local copies, waits for them, and re-layouts  1.48 us

profile of v2, /device:TPU:0, one launch (start us, length us, event | category | flops | bytes accessed | tf_op | source)
XLA Modules:
  0.0 46.1 jit_solution(8341163911353703553)
XLA Ops:
  0.0 0.8 %copy.7.mask_ref = s32[8,4]{1,0:T(8,128)S(1)} copy(s32[8,4]{0,1:T(4,128)} %param.7) | data formatting | bytes 256 | tf_op args[1]
  0.8 0.0 copy-start
  0.8 0.0 copy-start.1
  0.8 0.0 copy-start.2
  0.8 0.0 copy-start.3
  0.8 1.5 %reshape.6.raw_ref = bf16[64,8192]{1,0:T(8,128)(2,1)S(1)} reshape(bf16[8,4,2,8192]{3,2,1,0:T(2,128)(2,1)} %param.6) | data formatting | bytes 2097152 | tf_op jit(solution)/shard_map/reshape | solution.py:484
  2.3 0.0 copy-done
  2.3 0.0 copy-done.1
  2.3 0.0 copy-done.2
  2.3 0.0 copy-done.3
  2.4 43.0 %shard_map.64 = bf16[128,1024]{1,0:T(8,128)(2,1)S(1)} custom-call(bf16[64,8192]{1,0:T(8,128)(2,1)S(1)} %reshape.6.raw_ref, s32[8,4]{1,0:T(8,128)S(1)} %copy.7.mask_ref, s32[2,2]{1,0:T(2,128)S(1)} %copy-done, f32[2,4,1024]{2,1,0:T(4,128)S(1)} %copy-done.3, f32[2,64,1024]{2,1,0:T(8,128)S(1)} %copy-done.1, f32[2,32,1024]{2,1,0:T(8,128)S(1)} %copy-done.2), custom_call_target="tpu_custom_call" | custom-call | flops 4294967296 | bytes 4194304 | tf_op jit(solution)/shard_map/pallas_call | solution.py:446
  45.4 0.7 %copy.9 = bf16[2,8,8,1024]{3,2,1,0:T(8,128)(2,1)} copy(bf16[2,8,8,1024]{3,2,1,0:T(8,128)(2,1)S(1)} %bitcast.1) | data formatting | bytes 524288
Async XLA Ops:
  0.8 1.6 %copy-start = (s32[2,2]{1,0:T(2,128)S(1)}, s32[2,2]{1,0:T(2,128)}, u32[]{:S(2)}) copy-start(s32[2,2]{1,0:T(2,128)} %pair_ref.1) | copy-start | bytes 52
  0.8 1.6 %copy-start.1 = (f32[2,64,1024]{2,1,0:T(8,128)S(1)}, f32[2,64,1024]{2,1,0:T(8,128)}, u32[]{:S(2)}) copy-start(f32[2,64,1024]{2,1,0:T(8,128)} %constant.7.clone.coarse_table) | copy-start | bytes 1572868
  0.8 1.6 %copy-start.2 = (f32[2,32,1024]{2,1,0:T(8,128)S(1)}, f32[2,32,1024]{2,1,0:T(8,128)}, u32[]{:S(2)}) copy-start(f32[2,32,1024]{2,1,0:T(8,128)} %constant.8.clone.fine_table) | copy-start | bytes 786436
  0.8 1.6 %copy-start.3 = (f32[2,4,1024]{2,1,0:T(4,128)S(1)}, f32[2,4,1024]{2,1,0:T(4,128)}, u32[]{:S(2)}) copy-start(f32[2,4,1024]{2,1,0:T(4,128)} %constant.6.clone.rank_table) | copy-start | bytes 98308

commit v3 on v2

--- a/solution.py
+++ b/solution.py
@@ -12,7 +12,7 @@
 LAGS = 1024
 REACH = 2
 GROUP = 4
-CHUNKS = 8
+CHUNKS = 4
 LANES = 128
 FINE = 32
 MESH = pl.DeviceIdType.MESH
@@ -200,6 +200,9 @@
         ).astype(jnp.bfloat16)
         return carry
 
+    for index in range(CHUNKS):
+        lax.fori_loop(0, chunk // FINE, functools.partial(fill, index), 0)
+
     def forward(index):
         own_copy(index).wait()
         for step in steps:
@@ -316,7 +319,6 @@
     for index in range(CHUNKS):
         if index + 1 < CHUNKS:
             forward(index + 1)
-        lax.fori_loop(0, chunk // FINE, functools.partial(fill, index), 0)
         work(index)
 
     mine = slots * pairs

time: 46.3 us -> 43.2 us (0.933)
  Pallas kernels: 43 us -> 40 us
    pallas_call x1, Pallas kernels: 43 us -> 40 us  [shards(): pl.pallas_call(functools.partial(kernel, dims), out_shape=jax.ShapeDtypeS...]
where the time goes in v3:
time: 43.2 us; the launch traced here: 43.1 us
  Pallas kernels  40 us (93%)
  local copies, waits for them, and re-layouts  3.02 us (7%)
    pallas_call x1, Pallas kernels, shards(): pl.pallas_call(functools.partial(kernel, dims), out_shape=jax.ShapeDtypeS...  40 us
    reshape x1, local copies, waits for them, and re-layouts, shards(): spectra.reshape(rows, freqs)  1.54 us
    unnamed x10, local copies, waits for them, and re-layouts  1.48 us

profile of v3, /device:TPU:0, one launch (start us, length us, event | category | flops | bytes accessed | tf_op | source)
XLA Modules:
  0.0 43.1 jit_solution(2523236107588999855)
XLA Ops:
  0.0 0.8 %copy.7.mask_ref = s32[8,4]{1,0:T(8,128)S(1)} copy(s32[8,4]{0,1:T(4,128)} %param.7) | data formatting | bytes 256 | tf_op args[1]
  0.8 0.0 copy-start
  0.8 0.0 copy-start.1
  0.8 0.0 copy-start.2
  0.8 0.0 copy-start.3
  0.8 1.5 %reshape.6.raw_ref = bf16[64,8192]{1,0:T(8,128)(2,1)S(1)} reshape(bf16[8,4,2,8192]{3,2,1,0:T(2,128)(2,1)} %param.6) | data formatting | bytes 2097152 | tf_op jit(solution)/shard_map/reshape | solution.py:486
  2.3 0.0 copy-done
  2.3 0.0 copy-done.1
  2.3 0.0 copy-done.2
  2.3 0.0 copy-done.3
  2.4 40.0 %shard_map.64 = bf16[128,1024]{1,0:T(8,128)(2,1)S(1)} custom-call(bf16[64,8192]{1,0:T(8,128)(2,1)S(1)} %reshape.6.raw_ref, s32[8,4]{1,0:T(8,128)S(1)} %copy.7.mask_ref, s32[2,2]{1,0:T(2,128)S(1)} %copy-done, f32[2,4,1024]{2,1,0:T(4,128)S(1)} %copy-done.3, f32[2,64,1024]{2,1,0:T(8,128)S(1)} %copy-done.1, f32[2,32,1024]{2,1,0:T(8,128)S(1)} %copy-done.2), custom_call_target="tpu_custom_call" | custom-call | flops 4294967296 | bytes 4194304 | tf_op jit(solution)/shard_map/pallas_call | solution.py:448
  42.3 0.7 %copy.9 = bf16[2,8,8,1024]{3,2,1,0:T(8,128)(2,1)} copy(bf16[2,8,8,1024]{3,2,1,0:T(8,128)(2,1)S(1)} %bitcast.1) | data formatting | bytes 524288
Async XLA Ops:
  0.8 1.6 %copy-start = (s32[2,2]{1,0:T(2,128)S(1)}, s32[2,2]{1,0:T(2,128)}, u32[]{:S(2)}) copy-start(s32[2,2]{1,0:T(2,128)} %pair_ref.1) | copy-start | bytes 52
  0.8 1.6 %copy-start.1 = (f32[2,64,1024]{2,1,0:T(8,128)S(1)}, f32[2,64,1024]{2,1,0:T(8,128)}, u32[]{:S(2)}) copy-start(f32[2,64,1024]{2,1,0:T(8,128)} %constant.7.clone.coarse_table) | copy-start | bytes 1572868
  0.8 1.6 %copy-start.2 = (f32[2,32,1024]{2,1,0:T(8,128)S(1)}, f32[2,32,1024]{2,1,0:T(8,128)}, u32[]{:S(2)}) copy-start(f32[2,32,1024]{2,1,0:T(8,128)} %constant.8.clone.fine_table) | copy-start | bytes 786436
  0.8 1.6 %copy-start.3 = (f32[2,4,1024]{2,1,0:T(4,128)S(1)}, f32[2,4,1024]{2,1,0:T(4,128)}, u32[]{:S(2)}) copy-start(f32[2,4,1024]{2,1,0:T(4,128)} %constant.6.clone.rank_table) | copy-start | bytes 98308

commit v4 on v3

--- a/solution.py
+++ b/solution.py
@@ -253,11 +253,7 @@
         lax.fori_loop(0, held_blocks, widen, 0)
         cross = cross_of[index % 2]
 
-        def slot_cross(place_at, carry):
-            if index > 0:
-                product(
-                    index - 1, place_at % 2, pl.multiple_of((place_at // 2) * width, width)
-                )
+        def slot_cross(place_at):
             slot = place_at % slots
             owner = ((place_at // slots) % 2) * 2 + place_at // (2 * slots)
             left = place(slot_smem[owner, 0, slot * 2])
@@ -294,9 +290,25 @@
                     cross[at_row, pl.ds(chunk + column, LANES)] = jnp.concatenate(
                         imags, axis=0
                     ).astype(jnp.bfloat16)
+
+        def columns_and_slots(piece, carry):
+            if index > 0:
+                column = pl.ds(pl.multiple_of(piece * width, width), width)
+                part = jnp.dot(
+                    cross_of[(index - 1) % 2][...],
+                    table[index - 1, :, column],
+                    preferred_element_type=jnp.float32,
+                )
+                for k in range(2):
+                    rows_of = part[k * half : (k + 1) * half]
+                    if index > 1:
+                        rows_of = rows_of + total[k, :, column]
+                    total[k, :, column] = rows_of
+            slot_cross(piece * 2)
+            slot_cross(piece * 2 + 1)
             return carry
 
-        lax.fori_loop(0, GROUP * slots, slot_cross, 0)
+        lax.fori_loop(0, GROUP * slots // 2, columns_and_slots, 0)
 
     forward(0)
     for step in steps:

time: 43.2 us -> 41.8 us (0.968)
  Pallas kernels: 40 us -> 38.6 us
    pallas_call x1, Pallas kernels: 40 us -> 38.6 us  [shards(): pl.pallas_call(functools.partial(kernel, dims), out_shape=jax.ShapeDtypeS...]
where the time goes in v4:
time: 41.8 us; the launch traced here: 41.7 us
  Pallas kernels  38.6 us (92%)
  local copies, waits for them, and re-layouts  3.02 us (7%)
    pallas_call x1, Pallas kernels, shards(): pl.pallas_call(functools.partial(kernel, dims), out_shape=jax.ShapeDtypeS...  38.6 us
    reshape x1, local copies, waits for them, and re-layouts, shards(): spectra.reshape(rows, freqs)  1.54 us
    unnamed x10, local copies, waits for them, and re-layouts  1.48 us

profile of v4, /device:TPU:0, one launch (start us, length us, event | category | flops | bytes accessed | tf_op | source)
XLA Modules:
  0.0 41.7 jit_solution(15578191026331573263)
XLA Ops:
  0.0 0.8 %copy.7.mask_ref = s32[8,4]{1,0:T(8,128)S(1)} copy(s32[8,4]{0,1:T(4,128)} %param.7) | data formatting | bytes 256 | tf_op args[1]
  0.8 0.0 copy-start
  0.8 0.0 copy-start.1
  0.8 0.0 copy-start.2
  0.8 0.0 copy-start.3
  0.8 1.5 %reshape.6.raw_ref = bf16[64,8192]{1,0:T(8,128)(2,1)S(1)} reshape(bf16[8,4,2,8192]{3,2,1,0:T(2,128)(2,1)} %param.6) | data formatting | bytes 2097152 | tf_op jit(solution)/shard_map/reshape | solution.py:498
  2.3 0.0 copy-done
  2.3 0.0 copy-done.1
  2.3 0.0 copy-done.2
  2.3 0.0 copy-done.3
  2.4 38.6 %shard_map.64 = bf16[128,1024]{1,0:T(8,128)(2,1)S(1)} custom-call(bf16[64,8192]{1,0:T(8,128)(2,1)S(1)} %reshape.6.raw_ref, s32[8,4]{1,0:T(8,128)S(1)} %copy.7.mask_ref, s32[2,2]{1,0:T(2,128)S(1)} %copy-done, f32[2,4,1024]{2,1,0:T(4,128)S(1)} %copy-done.3, f32[2,64,1024]{2,1,0:T(8,128)S(1)} %copy-done.1, f32[2,32,1024]{2,1,0:T(8,128)S(1)} %copy-done.2), custom_call_target="tpu_custom_call" | custom-call | flops 4294967296 | bytes 4194304 | tf_op jit(solution)/shard_map/pallas_call | solution.py:460
  41.0 0.7 %copy.9 = bf16[2,8,8,1024]{3,2,1,0:T(8,128)(2,1)} copy(bf16[2,8,8,1024]{3,2,1,0:T(8,128)(2,1)S(1)} %bitcast.1) | data formatting | bytes 524288
Async XLA Ops:
  0.8 1.6 %copy-start = (s32[2,2]{1,0:T(2,128)S(1)}, s32[2,2]{1,0:T(2,128)}, u32[]{:S(2)}) copy-start(s32[2,2]{1,0:T(2,128)} %pair_ref.1) | copy-start | bytes 52
  0.8 1.6 %copy-start.1 = (f32[2,64,1024]{2,1,0:T(8,128)S(1)}, f32[2,64,1024]{2,1,0:T(8,128)}, u32[]{:S(2)}) copy-start(f32[2,64,1024]{2,1,0:T(8,128)} %constant.7.clone.coarse_table) | copy-start | bytes 1572868
  0.8 1.6 %copy-start.2 = (f32[2,32,1024]{2,1,0:T(8,128)S(1)}, f32[2,32,1024]{2,1,0:T(8,128)}, u32[]{:S(2)}) copy-start(f32[2,32,1024]{2,1,0:T(8,128)} %constant.8.clone.fine_table) | copy-start | bytes 786436
  0.8 1.6 %copy-start.3 = (f32[2,4,1024]{2,1,0:T(4,128)S(1)}, f32[2,4,1024]{2,1,0:T(4,128)}, u32[]{:S(2)}) copy-start(f32[2,4,1024]{2,1,0:T(4,128)} %constant.6.clone.rank_table) | copy-start | bytes 98308
